TPU v7x, 512 devices: a whole 4x8x8 slice. The times are simulated.
512 devices in a mesh: row: 16 (over z_hi, y), col: 32 (over x, z_lo, core).
Axes of the slice: x: 4, y: 8, z: 8 (z_hi: 2, z_lo: 4; z = z_hi * 4 + z_lo), core: 2. Of those that a mesh axis runs over, the one named last changes fastest.
Arguments:
- cov_tiles: float32 [2, 16, 1, 32, 512, 512], P(None, 'row', None, 'col'), may hold values from -6 to 6
- inverse_factors: float32 [2, 512, 512], P(None, 'row'), may hold values from -0.3 to 0.3, as said below
- band: int32 [32], replicated, may hold values from 1 to 24, as said below
- station_noise: float32 [16384], replicated, may hold values from 0.5 to 4
- morton: int32 [16384], replicated, may hold values from 0 to 16383, each once
Outputs:
- factor_window: float32 [2, 16, 1, 32, 512, 512], P(None, 'row', None, 'col')
Inputs may be any that keep to these rules, and one draw needn't show every extreme that they name: `inverse_factors`: each matrix is upper triangular with a positive diagonal. Some row of tiles has a band of exactly 24.
All inputs are finite; a program needn't handle non-finite values.
Results may differ from a plain program's by a relative error of at most 0.0003.
Values sent between devices are 32-bit elements; how exact they have to be, the bound alone decides.
A program may use at most 64 MiB of HBM per device.

v0:
```python
import jax
import jax.numpy as jnp
from jax import lax
from jax.sharding import PartitionSpec as P

STEPS = 2


def spread(value, axis, source):
    kept = jnp.where(lax.axis_index(axis) == source, value, 0).astype(value.dtype)
    return lax.psum(kept, axis)


def on_device(cov_tiles, inverse_factors, band, station_noise, morton):
    grid_rows = lax.axis_size("row")
    grid_cols = lax.axis_size("col")
    own_row = lax.axis_index("row")
    own_col = lax.axis_index("col")
    blocks = cov_tiles[:, 0, :, 0]
    tile_rows = blocks.shape[0]
    tile_cols = blocks.shape[1]
    tile_size = blocks.shape[2]
    tile_count = band.shape[0]
    row_ids = jnp.arange(tile_rows, dtype=jnp.int32) * grid_rows + own_row
    col_ids = jnp.arange(tile_cols, dtype=jnp.int32) * grid_cols + own_col
    every_tile = jnp.arange(tile_count, dtype=jnp.int32)
    row_band = jnp.sum(jnp.where(every_tile[None, :] == row_ids[:, None], band[None, :], 0), axis=1)
    kept_mask = (col_ids[None, :] <= row_ids[:, None]) & (
        row_ids[:, None] - col_ids[None, :] <= row_band[:, None]
    )
    blocks = jnp.where(kept_mask[:, :, None, None], blocks, 0.0)
    is_diagonal = col_ids[None, :] == row_ids[:, None]
    mirrored = jnp.tril(blocks) + jnp.swapaxes(jnp.tril(blocks, -1), -1, -2)
    station_rows = morton.reshape(tile_count, tile_size)[row_ids]
    nugget = station_noise[station_rows]
    identity = jnp.eye(tile_size, dtype=jnp.float32)
    mirrored = mirrored + nugget[:, None, :, None] * identity
    blocks = jnp.where(is_diagonal[:, :, None, None], mirrored, blocks)
    for panel_step in range(STEPS):
        factor = lax.all_gather(inverse_factors[panel_step], "row", axis=0, tiled=True)
        owner_col = panel_step % grid_cols
        owner_slot = panel_step // grid_cols

        def make_factor(column):
            return jnp.einsum(
                "amn,np->amp",
                column,
                factor,
                precision=lax.Precision.HIGHEST,
                preferred_element_type=jnp.float32,
            )

        column = blocks[:, owner_slot]
        row_factor = lax.cond(own_col == owner_col, make_factor, jnp.zeros_like, column)
        row_factor = jnp.where((row_ids > panel_step)[:, None, None], row_factor, 0.0)
        row_factor = spread(row_factor, "col", owner_col)
        blocks = blocks.at[:, owner_slot].set(jnp.where(own_col == owner_col, row_factor, column))
        target = 0 + own_col
        held_tile = lax.dynamic_index_in_dim(row_factor, target // grid_rows, 0, keepdims=False)
        pieces = [spread(held_tile, "row", target % grid_rows)]
        col_factor = jnp.stack(pieces)
        update = jnp.einsum(
            "amp,bnp->abmn",
            row_factor,
            col_factor,
            precision=lax.Precision.HIGHEST,
            preferred_element_type=jnp.float32,
        )
        active = (col_ids[None, :] > panel_step) & (col_ids[None, :] <= row_ids[:, None])
        blocks = blocks - jnp.where(active[:, :, None, None], update, 0.0)
    return blocks[:, None, :, None]


def solution(mesh):
    placed = (P(None, "row", None, "col", None, None), P(None, "row", None), P(), P(), P())
    return jax.shard_map(
        on_device,
        mesh=mesh,
        in_specs=placed,
        out_specs=P(None, "row", None, "col", None, None),
        check_vma=False,
    )
```

profile of v0, /device:TPU:2, one launch (start us, length us, event | category | flops | bytes accessed | tf_op | source)
XLA Modules:
  0.0 1189.5 jit_solution(2500794160252668181)
XLA Ops:
  6.5 0.0 copy-start
  6.5 0.0 all-gather.5.cloned.1.call-start
  6.5 1.6 fusion.13
  8.1 0.0 all-gather.5.cloned.1.call-update
  8.1 0.0 all-reduce.5.cloned.1.call-start
  8.2 0.8 fusion.11
  9.1 1.9 bitcast_select_fusion.2
  11.0 0.0 copy-start.4
  11.0 1.8 copy.21
  12.8 0.0 copy-done.4
  12.8 0.6 gather_fusion
  13.4 0.0 copy-done
  13.4 0.0 copy-start.1
  13.4 6.2 gather_fusion.1
  19.6 0.2 iota_compare_fusion.2
  19.8 0.2 iota_compare_fusion.1
  20.1 0.0 copy-done.1
  20.1 3.7 fusion.6
  23.7 2.9 copy.23
  26.7 3.5 select_bitcast_fusion
  30.1 78.5 %all-gather.5.cloned.1.call-done = f32[1,512,512]{2,1,0:T(8,128)} async-done(((f32[1,32,512]{2,1,0:T(8,128)}), f32[1,512,512]{2,1,0:T(8,128)}) %all-gather.5.cloned.1.call-update) | async-done | bytes 1048592 | tf_op jit(solution)/shard_map/all_gather | solution.py:40
  108.6 0.3 conditional.2
  108.6 0.2 broadcast.314
  108.9 1.7 select_select_fusion.1
  110.6 0.0 all-reduce.5.cloned.1.call-update
  110.6 0.0 copy-start.2
  110.6 0.0 all-reduce.7.cloned.1.call-start
  110.7 269.9 %all-reduce.5.cloned.1.call-done = f32[2,512,512]{2,1,0:T(8,128)} async-done(((f32[2,512,512]{2,1,0:T(8,128)}), f32[2,512,512]{2,1,0:T(8,128)}) %all-reduce.5.cloned.1.call-update) | async-done | bytes 2097168 | tf_op jit(solution)/shard_map/psum | solution.py:11
  380.6 2.3 select_bitcast_fusion.2
  382.9 0.0 all-reduce.7.cloned.1.call-update
  382.9 0.0 all-gather.7.cloned.1.call-start
  383.0 0.5 all-gather.7.cloned.1.call-update
  383.5 0.0 all-reduce.9.cloned.1.call-start
  383.6 211.9 %all-reduce.7.cloned.1.call-done = f32[512,512]{1,0:T(8,128)} async-done(((f32[512,512]{1,0:T(8,128)}), f32[512,512]{1,0:T(8,128)}) %all-reduce.7.cloned.1.call-update) | async-done | bytes 1048592 | tf_op jit(solution)/shard_map/psum | solution.py:11
  595.5 0.0 copy-done.2
  595.5 7.4 fusion.5
  602.9 86.3 %all-gather.7.cloned.1.call-done = f32[1,512,512]{2,1,0:T(8,128)} async-done(((f32[1,32,512]{2,1,0:T(8,128)}), f32[1,512,512]{2,1,0:T(8,128)}) %all-gather.7.cloned.1.call-update) | async-done | bytes 1048592 | tf_op jit(solution)/shard_map/all_gather | solution.py:40
  689.2 0.4 conditional.3
  689.2 0.2 broadcast.315
  689.7 1.7 select_select_fusion
  691.4 0.0 all-reduce.9.cloned.1.call-update
  691.4 0.0 copy-start.3
  691.5 0.0 all-reduce.11.cloned.1.call-start
  691.5 268.7 %all-reduce.9.cloned.1.call-done = f32[2,512,512]{2,1,0:T(8,128)} async-done(((f32[2,512,512]{2,1,0:T(8,128)}), f32[2,512,512]{2,1,0:T(8,128)}) %all-reduce.9.cloned.1.call-update) | async-done | bytes 2097168 | tf_op jit(solution)/shard_map/psum | solution.py:11
  960.3 2.3 select_bitcast_fusion.1
  962.6 0.0 all-reduce.11.cloned.1.call-update
  962.6 212.6 %all-reduce.11.cloned.1.call-done = f32[512,512]{1,0:T(8,128)} async-done(((f32[512,512]{1,0:T(8,128)}), f32[512,512]{1,0:T(8,128)}) %all-reduce.11.cloned.1.call-update) | async-done | bytes 1048592 | tf_op jit(solution)/shard_map/psum | solution.py:11
  1175.2 0.0 copy-done.3
  1175.2 7.4 fusion.4
  (14 shorter events, 0.1 us)
Async XLA Ops:
  6.5 6.9 copy-start
  6.5 102.1 %all-gather.5.cloned.1.call-start = ((), (), s32[]{:S(2)}) async-start(), calls=%async_computation.4 | async-start | bytes 1114112 | tf_op jit(solution)/shard_map/all_gather | solution.py:40
  8.1 372.5 %all-reduce.5.cloned.1.call-start = ((), (), s32[]{:S(2)}) async-start(), calls=%async_computation | async-start | bytes 4194304 | tf_op jit(solution)/shard_map/psum | solution.py:11
  11.0 1.8 copy-start.4
  13.4 6.6 copy-start.1
  110.6 484.9 %copy-start.2 = (f32[2,512,512]{2,1,0:T(8,128)S(1)}, f32[2,512,512]{2,1,0:T(8,128)}, u32[]{:S(2)}) copy-start(f32[2,512,512]{2,1,0:T(8,128)} %select_bitcast_fusion) | copy-start | bytes 6291460
  110.6 484.9 %all-reduce.7.cloned.1.call-start = ((), (), s32[]{:S(2)}) async-start(), calls=%async_computation.1 | async-start | bytes 2097152 | tf_op jit(solution)/shard_map/psum | solution.py:11
  382.9 306.3 %all-gather.7.cloned.1.call-start = ((), (), s32[]{:S(2)}) async-start(), calls=%async_computation.5 | async-start | bytes 1114112 | tf_op jit(solution)/shard_map/all_gather | solution.py:40
  383.5 576.7 %all-reduce.9.cloned.1.call-start = ((), (), s32[]{:S(2)}) async-start(), calls=%async_computation.2 | async-start | bytes 4194304 | tf_op jit(solution)/shard_map/psum | solution.py:11
  691.4 483.8 %copy-start.3 = (f32[2,512,512]{2,1,0:T(8,128)S(1)}, f32[2,512,512]{2,1,0:T(8,128)}, u32[]{:S(2)}) copy-start(f32[2,512,512]{2,1,0:T(8,128)} %fusion.5) | copy-start | bytes 6291460
  691.5 483.8 %all-reduce.11.cloned.1.call-start = ((), (), s32[]{:S(2)}) async-start(), calls=%async_computation.3 | async-start | bytes 2097152 | tf_op jit(solution)/shard_map/psum | solution.py:11
Sparse Core Ops, SparseCore 0:
  10.6 97.9 all-gather.4
  111.5 269.0 all-reduce.4
  383.8 211.6 all-reduce.6
  598.6 90.6 all-gather.6
  692.0 268.2 all-reduce.8
  963.3 211.8 all-reduce.10
where the time goes:
time: 1190 us
  waiting for transfers between devices  1130 us (95%)
  other arithmetic  18.4 us (2%)
  matrix products  14.8 us (1%)
  between operations  13.7 us (1%)
  local copies, waits for them, and re-layouts  13.5 us (1%)
    psum x4, waiting for transfers between devices, spread(): return lax.psum(kept, axis)  963 us
    all_gather x2, waiting for transfers between devices, on_device(): lax.all_gather(inverse_factors[panel_step], 'row', axis=0, tiled=True)  165 us
  transfers between devices with their start and end apart: 6, of which 6 were waited for; matrix products, arithmetic and copies ran while one was open for 2% of the time, Pallas kernels for 0%

commit v1 on v0

--- a/solution.py
+++ b/solution.py
@@ -37,7 +37,11 @@
     mirrored = mirrored + nugget[:, None, :, None] * identity
     blocks = jnp.where(is_diagonal[:, :, None, None], mirrored, blocks)
     for panel_step in range(STEPS):
-        factor = lax.all_gather(inverse_factors[panel_step], "row", axis=0, tiled=True)
+        x = inverse_factors[panel_step]
+        devices = lax.axis_size("row")
+        parts = jnp.stack([x for _ in range(devices)])
+        parts = lax.all_to_all(parts, "row", split_axis=0, concat_axis=0)
+        factor = jnp.concatenate(parts, axis=0)
         owner_col = panel_step % grid_cols
         owner_slot = panel_step // grid_cols
 

time: 1190 us -> 1070 us (0.90)
  waiting for transfers between devices: 1130 us -> 988 us
  starting transfers between devices: 0.21 us -> 23 us
    all_gather x2 -> x0, waiting for transfers between devices: 165 us -> none  [on_device(): lax.all_gather(inverse_factors[panel_step], 'row', axis=0, tiled=True)]
    all_to_all x0 -> x2, starting transfers between devices: none -> 22.9 us  [on_device(): parts = lax.all_to_all(parts, 'row', split_axis=0, concat_axis=0)]
    psum x4, waiting for transfers between devices: 963 us -> 979 us  [spread(): return lax.psum(kept, axis)]
  transfers between devices with their start and end apart: 6 -> 6, of which waited for: 6 -> 5; matrix products, arithmetic and copies ran while one was open for 2% -> 3% of each run, Pallas kernels for 0% -> 0%
where the time goes in v1:
time: 1070 us
  waiting for transfers between devices  988 us (92%)
  starting transfers between devices  23 us (2%)
  other arithmetic  17.5 us (2%)
  local copies, waits for them, and re-layouts  16.3 us (2%)
  matrix products  14.8 us (1%)
  between operations  13.4 us (1%)
    psum x4, waiting for transfers between devices, spread(): return lax.psum(kept, axis)  979 us
    all_to_all x2, starting transfers between devices, on_device(): parts = lax.all_to_all(parts, 'row', split_axis=0, concat_axis=0)  22.9 us
  transfers between devices with their start and end apart: 6, of which 5 were waited for; matrix products, arithmetic and copies ran while one was open for 3% of the time, Pallas kernels for 0%

profile of v1, /device:TPU:2, one launch (start us, length us, event | category | flops | bytes accessed | tf_op | source)
XLA Modules:
  0.0 1073.3 jit_solution(18370270077272132258)
XLA Ops:
  6.5 0.0 copy-start
  6.5 0.0 copy-start.5
  6.5 0.0 copy-start.1
  6.5 1.0 slice_bitcast_fusion
  7.6 1.1 stack.9
  8.7 15.6 %all-to-all-start.1 = ((f32[16,32,512]{2,1,0:T(8,128)}), f32[16,32,512]{2,1,0:T(8,128)S(1)}, u32[]{:S(2)}, u32[]{:S(2)}) async-start(f32[16,32,512]{2,1,0:T(8,128)} %stack.9), calls=%async_computation.1 | async-start | bytes 2097152 | tf_op jit(solution)/shard_map/all_to_all | solution.py:43
  24.3 0.0 all-reduce.5.cloned.1.call-start
  24.4 0.0 copy-done.5
  24.4 0.2 fusion.7
  24.6 0.0 copy-done.1
  24.6 1.6 bitcast_select_fusion.2
  26.3 0.0 copy-start.4
  26.3 2.9 copy.21
  29.2 0.0 copy-done.4
  29.2 0.6 gather_fusion
  29.8 0.0 copy-done
  29.8 6.2 gather_fusion.1
  36.0 0.2 iota_compare_fusion.2
  36.2 0.2 iota_compare_fusion.1
  36.4 3.7 fusion.2
  40.1 2.9 copy.23
  43.0 3.5 select_bitcast_fusion
  46.5 9.2 all-to-all-done.1
  55.7 0.3 conditional.2
  55.7 0.2 broadcast.316
  55.9 1.7 select_select_fusion.1
  57.7 0.0 all-reduce.5.cloned.1.call-update
  57.7 1.1 stack.8
  58.8 7.2 all-to-all-start
  66.0 0.0 copy-start.2
  66.0 0.0 all-reduce.7.cloned.1.call-start
  66.1 281.2 %all-reduce.5.cloned.1.call-done = f32[2,512,512]{2,1,0:T(8,128)} async-done(((f32[2,512,512]{2,1,0:T(8,128)}), f32[2,512,512]{2,1,0:T(8,128)}) %all-reduce.5.cloned.1.call-update) | async-done | bytes 2097168 | tf_op jit(solution)/shard_map/psum | solution.py:11
  347.3 2.3 select_bitcast_fusion.2
  349.7 0.0 all-reduce.7.cloned.1.call-update
  349.7 0.0 all-reduce.9.cloned.1.call-start
  349.8 212.8 %all-reduce.7.cloned.1.call-done = f32[512,512]{1,0:T(8,128)} async-done(((f32[512,512]{1,0:T(8,128)}), f32[512,512]{1,0:T(8,128)}) %all-reduce.7.cloned.1.call-update) | async-done | bytes 1048592 | tf_op jit(solution)/shard_map/psum | solution.py:11
  562.5 0.0 copy-done.2
  562.5 7.4 fusion.1
  569.9 0.0 all-to-all-done
  569.9 0.4 conditional.3
  569.9 0.2 broadcast.317
  570.4 1.7 select_select_fusion
  572.1 0.0 all-reduce.9.cloned.1.call-update
  572.1 0.0 copy-start.3
  572.1 0.0 all-reduce.11.cloned.1.call-start
  572.2 272.3 %all-reduce.9.cloned.1.call-done = f32[2,512,512]{2,1,0:T(8,128)} async-done(((f32[2,512,512]{2,1,0:T(8,128)}), f32[2,512,512]{2,1,0:T(8,128)}) %all-reduce.9.cloned.1.call-update) | async-done | bytes 2097168 | tf_op jit(solution)/shard_map/psum | solution.py:11
  844.4 2.3 select_bitcast_fusion.1
  846.8 0.0 all-reduce.11.cloned.1.call-update
  846.8 212.6 %all-reduce.11.cloned.1.call-done = f32[512,512]{1,0:T(8,128)} async-done(((f32[512,512]{1,0:T(8,128)}), f32[512,512]{1,0:T(8,128)}) %all-reduce.11.cloned.1.call-update) | async-done | bytes 1048592 | tf_op jit(solution)/shard_map/psum | solution.py:11
  1059.4 0.0 copy-done.3
  1059.4 7.4 fusion
  (13 shorter events, 0.1 us)
Async XLA Ops:
  6.5 23.3 %copy-start = (f32[16384]{0:T(1024)S(1)}, f32[16384]{0:T(1024)}, u32[]{:S(2)}) copy-start(f32[16384]{0:T(1024)} %param.16) | copy-start | bytes 196612
  6.5 17.9 %copy-start.5 = (s32[32]{0:T(128)S(1)}, s32[32]{0:T(128)}, u32[]{:S(2)}) copy-start(s32[32]{0:T(128)} %param.15) | copy-start | bytes 388
  6.5 18.1 %copy-start.1 = (f32[2,1,1,1,512,512]{5,4,3,2,1,0:T(8,128)S(1)}, f32[2,1,1,1,512,512]{5,4,3,2,1,0:T(8,128)}, u32[]{:S(2)}) copy-start(f32[2,1,1,1,512,512]{5,4,3,2,1,0:T(8,128)} %param.13) | copy-start | bytes 6291460
  8.7 47.0 %all-to-all-start.1 = ((f32[16,32,512]{2,1,0:T(8,128)}), f32[16,32,512]{2,1,0:T(8,128)S(1)}, u32[]{:S(2)}, u32[]{:S(2)}) async-start(f32[16,32,512]{2,1,0:T(8,128)} %stack.9), calls=%async_computation.1 | async-start | bytes 2097152 | tf_op jit(solution)/shard_map/all_to_all | solution.py:43
  24.3 323.0 %all-reduce.5.cloned.1.call-start = ((), (), s32[]{:S(2)}) async-start(), calls=%async_computation.2 | async-start | bytes 4194304 | tf_op jit(solution)/shard_map/psum | solution.py:11
  26.3 2.9 copy-start.4
  58.8 511.1 %all-to-all-start = ((f32[16,32,512]{2,1,0:T(8,128)}), f32[16,32,512]{2,1,0:T(8,128)S(1)}, u32[]{:S(2)}, u32[]{:S(2)}) async-start(f32[16,32,512]{2,1,0:T(8,128)} %stack.8), calls=%async_computation | async-start | bytes 2097152 | tf_op jit(solution)/shard_map/all_to_all | solution.py:43
  66.0 496.5 %copy-start.2 = (f32[2,512,512]{2,1,0:T(8,128)S(1)}, f32[2,512,512]{2,1,0:T(8,128)}, u32[]{:S(2)}) copy-start(f32[2,512,512]{2,1,0:T(8,128)} %select_bitcast_fusion) | copy-start | bytes 6291460
  66.0 496.5 %all-reduce.7.cloned.1.call-start = ((), (), s32[]{:S(2)}) async-start(), calls=%async_computation.3 | async-start | bytes 2097152 | tf_op jit(solution)/shard_map/psum | solution.py:11
  349.7 494.8 %all-reduce.9.cloned.1.call-start = ((), (), s32[]{:S(2)}) async-start(), calls=%async_computation.4 | async-start | bytes 4194304 | tf_op jit(solution)/shard_map/psum | solution.py:11
  572.1 487.3 %copy-start.3 = (f32[2,512,512]{2,1,0:T(8,128)S(1)}, f32[2,512,512]{2,1,0:T(8,128)}, u32[]{:S(2)}) copy-start(f32[2,512,512]{2,1,0:T(8,128)} %fusion.1) | copy-start | bytes 6291460
  572.1 487.3 %all-reduce.11.cloned.1.call-start = ((), (), s32[]{:S(2)}) async-start(), calls=%async_computation.5 | async-start | bytes 2097152 | tf_op jit(solution)/shard_map/psum | solution.py:11
Sparse Core Ops, SparseCore 0:
  57.8 289.4 all-reduce.4
  350.5 211.9 all-reduce.6
  572.2 272.1 all-reduce.8
  847.5 211.8 all-reduce.10
